TPU v7x, 32 devices: a whole 2x2x4 slice. The times are simulated.
32 devices in a mesh: fsdp: 4 (over y, core), expert: 8 (over z, x).
Axes of the slice: x: 2, y: 2, z: 4, core: 2. Of those that a mesh axis runs over, the one named last changes fastest.
Arguments:
- tokens: bfloat16 [4096, 1024], P(('fsdp', 'expert')), may hold values from -6 to 6
- expert_ids: int32 [4096, 2], P(('fsdp', 'expert')), may hold values from 0 to 7, all different within a row; in each aligned block of 128 rows (0 to 127, 128 to 255, ...) at most 64 rows name the same one
- gate_weights: float32 [4096, 2], P(('fsdp', 'expert')), may hold values from 0.2 to 1
- weight_in: bfloat16 [8, 2048, 1024], P('expert', 'fsdp'), may hold values from -0.1875 to 0.1875
- weight_out: bfloat16 [8, 2048, 1024], P('expert', 'fsdp'), may hold values from -0.125 to 0.125
- cotangent: bfloat16 [4096, 1024], P(('fsdp', 'expert')), may hold values from -3 to 3
Outputs:
- layer_out: bfloat16 [4096, 1024], P(('fsdp', 'expert'))
- token_grad: bfloat16 [4096, 1024], P(('fsdp', 'expert'))
- grad_in: float32 [8, 2048, 1024], P('expert', 'fsdp')
- grad_out: float32 [8, 2048, 1024], P('expert', 'fsdp')
Inputs may be any that keep to these rules, and one draw needn't show every extreme that they name: `expert_ids`: the two experts of a token differ. Among the 128 tokens of one device no expert is chosen by more than 64 tokens, and some device has an expert chosen by exactly 64 tokens.
All inputs are finite; a program needn't handle non-finite values.
Results may differ from a plain program's by a relative error of at most 0.014.
Values may be sent and summed in bfloat16 or wider, within the bound.
A program may use at most 128 MiB of HBM per device.

v0:
```python
import jax
import jax.numpy as jnp
from jax import lax
from jax.sharding import PartitionSpec as P


def gelu_back(pre_act, upstream):
    _, pullback = jax.vjp(jax.nn.gelu, pre_act)
    return pullback(upstream)[0]


def per_device(tokens, expert_ids, gate_weights, weight_in, weight_out, cotangent):
    tok_count, width = tokens.shape
    expert_count = lax.axis_size("expert")
    capacity = 4 * tok_count // expert_count
    labels = jnp.arange(expert_count, dtype=jnp.int32)
    hit_count = jnp.sum(
        (expert_ids[:, :, None] == labels).astype(jnp.int32), axis=1, dtype=jnp.int32
    )
    earlier = jnp.cumsum(hit_count, axis=0, dtype=jnp.int32) - hit_count
    slot_ids = jnp.take_along_axis(earlier, expert_ids, axis=1)
    target = expert_ids * capacity + slot_ids
    cell_ids = jnp.arange(expert_count * capacity, dtype=jnp.int32)[:, None]
    first_hit = cell_ids == target[:, 0][None, :]
    second_hit = cell_ids == target[:, 1][None, :]
    placing = (first_hit | second_hit).astype(jnp.bfloat16)
    gate_cells = jnp.sum(
        jnp.where(first_hit, gate_weights[:, 0][None, :], 0.0)
        + jnp.where(second_hit, gate_weights[:, 1][None, :], 0.0),
        axis=1,
    )
    outgoing = jnp.dot(placing, tokens, preferred_element_type=jnp.float32).astype(jnp.bfloat16)
    arrived = lax.all_to_all(
        outgoing.reshape(expert_count, capacity, width),
        "expert",
        split_axis=0,
        concat_axis=0,
        tiled=True,
    )
    expert_rows = arrived.reshape(-1, width)
    pieces = (
        lax.all_gather(weight_in, "fsdp", axis=1, tiled=True),
        lax.all_gather(weight_out, "fsdp", axis=1, tiled=True),
    )
    full_in = None
    full_out = None
    part_in = pieces[0][0]
    part_out = pieces[1][0]
    activation = lax.dot_general(
        expert_rows, part_in, (((1,), (1,)), ((), ())), preferred_element_type=jnp.float32
    )
    hidden = jax.nn.gelu(activation).astype(jnp.bfloat16)
    summed = jnp.dot(hidden, part_out, preferred_element_type=jnp.float32)
    forward_stored = activation.astype(jnp.bfloat16)
    summed, stored, hidden_buf, full_in, full_out = (
        summed,
        forward_stored,
        hidden,
        full_in,
        full_out,
    )
    expert_out = summed.astype(jnp.bfloat16).reshape(expert_count, capacity, width)
    returned = lax.all_to_all(
        expert_out, "expert", split_axis=0, concat_axis=0, tiled=True
    ).reshape(-1, width)
    picked = returned[target].astype(jnp.float32)
    layer_out = jnp.sum(picked * gate_weights[:, :, None], axis=1).astype(jnp.bfloat16)
    grad_cells = (
        jnp.dot(placing, cotangent, preferred_element_type=jnp.float32) * gate_cells[:, None]
    )
    grad_cells = grad_cells.astype(jnp.bfloat16).reshape(expert_count, capacity, width)
    grad_rows = lax.all_to_all(
        grad_cells, "expert", split_axis=0, concat_axis=0, tiled=True
    ).reshape(-1, width)
    pieces = (
        lax.all_gather(weight_in, "fsdp", axis=1, tiled=True),
        lax.all_gather(weight_out, "fsdp", axis=1, tiled=True),
    )
    part_in = pieces[0][0]
    part_out = pieces[1][0]
    grad_hidden = lax.dot_general(
        grad_rows, part_out, (((1,), (1,)), ((), ())), preferred_element_type=jnp.float32
    )
    pre_act = stored.astype(jnp.float32)
    grad_act = gelu_back(pre_act, grad_hidden).astype(jnp.bfloat16)
    summed_grad = jnp.dot(grad_act, part_in, preferred_element_type=jnp.float32)
    summed_grad, grad_act_buf = (summed_grad, grad_act)
    grad_back = summed_grad.astype(jnp.bfloat16).reshape(expert_count, capacity, width)
    grad_returned = lax.all_to_all(
        grad_back, "expert", split_axis=0, concat_axis=0, tiled=True
    ).reshape(-1, width)
    token_grad = jnp.sum(grad_returned[target].astype(jnp.float32), axis=1).astype(jnp.bfloat16)
    both_shards = lax.psum_scatter(
        jnp.concatenate(
            [
                lax.dot_general(
                    grad_act_buf,
                    expert_rows,
                    (((0,), (0,)), ((), ())),
                    preferred_element_type=jnp.float32,
                ),
                lax.dot_general(
                    hidden_buf,
                    grad_rows,
                    (((0,), (0,)), ((), ())),
                    preferred_element_type=jnp.float32,
                ),
            ],
            axis=1,
        ).astype(jnp.bfloat16),
        "fsdp",
        scatter_dimension=0,
        tiled=True,
    ).astype(jnp.float32)
    grad_in_shard = both_shards[:, :width]
    grad_out_shard = both_shards[:, width:]
    return (layer_out, token_grad, grad_in_shard[None], grad_out_shard[None])


def solution(mesh):
    return jax.shard_map(
        per_device,
        mesh=mesh,
        in_specs=(
            P(("fsdp", "expert"), None),
            P(("fsdp", "expert"), None),
            P(("fsdp", "expert"), None),
            P("expert", "fsdp", None),
            P("expert", "fsdp", None),
            P(("fsdp", "expert"), None),
        ),
        out_specs=(
            P(("fsdp", "expert"), None),
            P(("fsdp", "expert"), None),
            P("expert", "fsdp", None),
            P("expert", "fsdp", None),
        ),
        check_vma=False,
    )
```

profile of v0, /device:TPU:0, one launch (start us, length us, event | category | flops | bytes accessed | tf_op | source)
XLA Modules:
  0.0 193.5 jit_solution(12775202458178157617)
XLA Ops:
  10.6 1.9 %gather_fusion.2 = s32[256]{0:T(256)S(1)} fusion(s32[128,8]{1,0:T(8,128)S(1)} %sub.6, s32[256]{0:T(256)S(1)} %reshape.73), kind=kCustom, calls=%fused_computation.2 | custom fusion | bytes 4096 | tf_op jit(solution)/shard_map/jit(take_along_axis)/gather | solution.py:21
  12.8 1.4 convolution_convert_fusion.2
  14.2 7.2 %all-to-all-start = ((bf16[8,64,1024]{2,1,0:T(8,128)(2,1)}), bf16[8,64,1024]{2,1,0:T(8,128)(2,1)S(1)}, u32[]{:S(2)}, u32[]{:S(2)}) async-start(bf16[8,64,1024]{2,1,0:T(8,128)(2,1)} %bitcast.3), calls=%async_computation | async-start | bytes 2097152 | tf_op jit(solution)/shard_map/all_to_all | solution.py:33
  21.7 1.4 multiply_convert_fusion
  23.1 24.2 %all-to-all-done = bf16[8,64,1024]{2,1,0:T(8,128)(2,1)S(1)} async-done(((bf16[8,64,1024]{2,1,0:T(8,128)(2,1)}), bf16[8,64,1024]{2,1,0:T(8,128)(2,1)S(1)}, u32[]{:S(2)}, u32[]{:S(2)}) %all-to-all-start) | async-done | bytes 1048608 | tf_op jit(solution)/shard_map/all_to_all | solution.py:33
  47.3 3.6 %all-to-all-start.2 = ((bf16[8,64,1024]{2,1,0:T(8,128)(2,1)}), bf16[8,64,1024]{2,1,0:T(8,128)(2,1)S(1)}, u32[]{:S(2)}, u32[]{:S(2)}) async-start(bf16[8,64,1024]{2,1,0:T(8,128)(2,1)} %bitcast.11), calls=%async_computation.2 | async-start | bytes 2097152 | tf_op jit(solution)/shard_map/all_to_all | solution.py:72
  50.9 6.7 %fusion.23 = f32[512,2048]{1,0:T(8,128)} fusion(bf16[512,1024]{1,0:T(8,128)(2,1)S(1)} %bitcast.50, bf16[1,2048,1024]{2,1,0:T(8,128)(2,1)} %all-gather.3.cloned.1.call-done), kind=kOutput, calls=%fused_computation.32 | convolution fusion | flops 2147483648 | bytes 9437184 | tf_op jit(solution)/shard_map/dot_general | solution.py:49
  57.6 19.2 %all-to-all-done.2 = bf16[8,64,1024]{2,1,0:T(8,128)(2,1)S(1)} async-done(((bf16[8,64,1024]{2,1,0:T(8,128)(2,1)}), bf16[8,64,1024]{2,1,0:T(8,128)(2,1)S(1)}, u32[]{:S(2)}, u32[]{:S(2)}) %all-to-all-start.2) | async-done | bytes 1048608 | tf_op jit(solution)/shard_map/all_to_all | solution.py:72
  76.8 6.7 %convolution_convert_fusion = bf16[2048,1024]{0,1:T(8,128)(2,1)} fusion(bf16[512,1024]{1,0:T(8,128)(2,1)S(1)} %bitcast.52, f32[512,2048]{1,0:T(8,128)} %fusion.23), kind=kOutput, calls=%fused_computation.34 | convolution fusion | flops 2159017984 | bytes 9437184 | tf_op jit(solution)/shard_map/dot_general | solution.py:102
  83.5 7.5 %fusion.3 = bf16[512,2048]{1,0:T(8,128)(2,1)S(1)} fusion(bf16[512,1024]{1,0:T(8,128)(2,1)S(1)} %bitcast.53, bf16[1,2048,1024]{2,1,0:T(8,128)(2,1)} %all-gather.5.cloned.1.call-done, f32[512,2048]{1,0:T(8,128)} %fusion.23), kind=kOutput, calls=%fused_computation.12 | convolution fusion | flops 2170552320 | bytes 11534336 | tf_op jit(solution)/shard_map/dot_general | solution.py:81
  92.3 4.4 %convolution_convert_fusion.1 = bf16[2048,1024]{0,1:T(8,128)(2,1)} fusion(bf16[512,2048]{1,0:T(8,128)(2,1)S(1)} %fusion.3, bf16[512,1024]{1,0:T(8,128)(2,1)S(1)} %bitcast.51), kind=kOutput, calls=%fused_computation.35 | convolution fusion | flops 2149580800 | bytes 7340032 | tf_op jit(solution)/shard_map/dot_general | solution.py:96
  96.6 8.4 %pad_maximum_fusion = bf16[2048,2048]{0,1:T(8,128)(2,1)} fusion(bf16[2048,1024]{0,1:T(8,128)(2,1)} %convolution_convert_fusion, bf16[2048,1024]{0,1:T(8,128)(2,1)} %convolution_convert_fusion.1), kind=kLoop, calls=%fused_computation.3 | loop fusion | flops 16777216 | bytes 16777216 | tf_op jit(solution)/shard_map/concatenate | solution.py:94
  105.0 7.1 %fusion.30 = bf16[512,1024]{1,0:T(8,128)(2,1)} fusion(bf16[1,2048,1024]{2,1,0:T(8,128)(2,1)} %all-gather.5.cloned.1.call-done, f32[512,2048]{1,0:T(8,128)} %fusion.23), kind=kOutput, calls=%fused_computation.41 | convolution fusion | flops 2157445120 | bytes 9437184 | tf_op jit(solution)/shard_map/dot_general | solution.py:53
  112.1 4.9 %all-to-all-start.1 = ((bf16[8,64,1024]{2,1,0:T(8,128)(2,1)}), bf16[8,64,1024]{2,1,0:T(8,128)(2,1)S(1)}, u32[]{:S(2)}, u32[]{:S(2)}) async-start(bf16[8,64,1024]{2,1,0:T(8,128)(2,1)} %bitcast.7), calls=%async_computation.1 | async-start | bytes 2097152 | tf_op jit(solution)/shard_map/all_to_all | solution.py:63
  117.0 7.1 %fusion.27 = bf16[512,1024]{1,0:T(8,128)(2,1)} fusion(bf16[512,2048]{1,0:T(8,128)(2,1)} %copy-done.4, bf16[1,2048,1024]{2,1,0:T(8,128)(2,1)} %all-gather.3.cloned.1.call-done), kind=kOutput, calls=%fused_computation.40 | convolution fusion | flops 2148007936 | bytes 7340032 | tf_op jit(solution)/shard_map/dot_general | solution.py:86
  124.1 19.1 %all-to-all-done.1 = bf16[8,64,1024]{2,1,0:T(8,128)(2,1)S(1)} async-done(((bf16[8,64,1024]{2,1,0:T(8,128)(2,1)}), bf16[8,64,1024]{2,1,0:T(8,128)(2,1)S(1)}, u32[]{:S(2)}, u32[]{:S(2)}) %all-to-all-start.1) | async-done | bytes 1048608 | tf_op jit(solution)/shard_map/all_to_all | solution.py:63
  143.2 3.8 %all-to-all-start.3 = ((bf16[8,64,1024]{2,1,0:T(8,128)(2,1)}), bf16[8,64,1024]{2,1,0:T(8,128)(2,1)S(1)}, u32[]{:S(2)}, u32[]{:S(2)}) async-start(bf16[8,64,1024]{2,1,0:T(8,128)(2,1)} %bitcast.13), calls=%async_computation.3 | async-start | bytes 2097152 | tf_op jit(solution)/shard_map/all_to_all | solution.py:89
  149.2 23.6 %all-to-all-done.3 = bf16[8,64,1024]{2,1,0:T(8,128)(2,1)S(1)} async-done(((bf16[8,64,1024]{2,1,0:T(8,128)(2,1)}), bf16[8,64,1024]{2,1,0:T(8,128)(2,1)S(1)}, u32[]{:S(2)}, u32[]{:S(2)}) %all-to-all-start.3) | async-done | bytes 1048608 | tf_op jit(solution)/shard_map/all_to_all | solution.py:89
  174.2 2.1 %reduce_sum.42 = bf16[128,1024]{1,0:T(8,128)(2,1)} reduce(bf16[128,2,1024]{2,1,0:T(2,128)(2,1)S(1)} %reshape.70, bf16[]{:T(256)} %constant.40.clone.1), dimensions={1}, to_apply=%region_4.5 | reduce | flops 131072 | bytes 786434 | tf_op jit(solution)/shard_map/reduce_sum | solution.py:92
  176.3 2.1 %multiply_reduce_fusion = bf16[128,1024]{1,0:T(8,128)(2,1)} fusion(f32[128,2,1024]{2,1,0:T(2,128)S(1)} %reshape.83, f32[128,2]{1,0:T(8,128)S(1)} %copy.53), kind=kLoop, calls=%fused_computation.42 | loop fusion | flops 393216 | bytes 1311744 | tf_op jit(solution)/shard_map/reduce_sum | solution.py:67
  178.4 2.2 %convert_element_type.51 = f32[512,2048]{0,1:T(8,128)S(1)} convert(bf16[512,2048]{0,1:T(8,128)(2,1)} %reduce-scatter.2.cloned.1.call-done) | non-fusion elementwise | flops 1048576 | bytes 6291456 | tf_op jit(solution)/shard_map/convert_element_type | solution.py:114
  180.6 1.8 slice_bitcast_fusion
  182.3 2.9 %copy.54 = f32[1,512,1024]{2,1,0:T(8,128)} copy(f32[1,512,1024]{1,2,0:T(8,128)} %get-tuple-element.27) | data formatting | bytes 4194304
  185.2 1.8 copy.55
  (40 shorter events, 8.7 us)
Async XLA Ops:
  7.2 5.7 %copy-start = (bf16[128,1024]{1,0:T(8,128)(2,1)S(1)}, bf16[128,1024]{1,0:T(8,128)(2,1)}, u32[]{:S(2)}) copy-start(bf16[128,1024]{1,0:T(8,128)(2,1)} %param.6) | copy-start | bytes 786436
  7.2 43.7 %all-gather.3.cloned.1.call-start = ((), (), s32[]{:S(2)}) async-start(), calls=%async_computation.5 | async-start | bytes 5242880 | tf_op jit(solution)/shard_map/all_gather | solution.py:42
  7.9 75.6 %all-gather.5.cloned.1.call-start = ((), (), s32[]{:S(2)}) async-start(), calls=%async_computation.6 | async-start | bytes 5242880 | tf_op jit(solution)/shard_map/all_gather | solution.py:43
  10.6 2.2 %copy-start.2 = (s32[128,2]{0,1:T(2,128)S(1)}, s32[128,2]{0,1:T(2,128)}, u32[]{:S(2)}) copy-start(s32[128,2]{0,1:T(2,128)} %param.7) | copy-start | bytes 3076
  10.6 10.9 %copy-start.3 = (f32[128,2]{0,1:T(2,128)S(1)}, f32[128,2]{0,1:T(2,128)}, u32[]{:S(2)}) copy-start(f32[128,2]{0,1:T(2,128)} %param.8) | copy-start | bytes 3076
  10.6 11.0 %copy-start.1 = (bf16[128,1024]{1,0:T(8,128)(2,1)S(1)}, bf16[128,1024]{1,0:T(8,128)(2,1)}, u32[]{:S(2)}) copy-start(bf16[128,1024]{1,0:T(8,128)(2,1)} %param.11) | copy-start | bytes 786436
  14.2 33.0 %all-to-all-start = ((bf16[8,64,1024]{2,1,0:T(8,128)(2,1)}), bf16[8,64,1024]{2,1,0:T(8,128)(2,1)S(1)}, u32[]{:S(2)}, u32[]{:S(2)}) async-start(bf16[8,64,1024]{2,1,0:T(8,128)(2,1)} %bitcast.3), calls=%async_computation | async-start | bytes 2097152 | tf_op jit(solution)/shard_map/all_to_all | solution.py:33
  47.3 29.5 %all-to-all-start.2 = ((bf16[8,64,1024]{2,1,0:T(8,128)(2,1)}), bf16[8,64,1024]{2,1,0:T(8,128)(2,1)S(1)}, u32[]{:S(2)}, u32[]{:S(2)}) async-start(bf16[8,64,1024]{2,1,0:T(8,128)(2,1)} %bitcast.11), calls=%async_computation.2 | async-start | bytes 2097152 | tf_op jit(solution)/shard_map/all_to_all | solution.py:72
  50.8 127.5 %reduce-scatter.2.cloned.1.call-start = ((), (), s32[]{:S(2)}) async-start(), calls=%async_computation.7 | async-start | bytes 10485760 | tf_op jit(solution)/shard_map/reduce_scatter | solution.py:93
  90.9 1.3 copy-start.4
  112.1 31.1 %all-to-all-start.1 = ((bf16[8,64,1024]{2,1,0:T(8,128)(2,1)}), bf16[8,64,1024]{2,1,0:T(8,128)(2,1)S(1)}, u32[]{:S(2)}, u32[]{:S(2)}) async-start(bf16[8,64,1024]{2,1,0:T(8,128)(2,1)} %bitcast.7), calls=%async_computation.1 | async-start | bytes 2097152 | tf_op jit(solution)/shard_map/all_to_all | solution.py:63
  143.2 29.6 %all-to-all-start.3 = ((bf16[8,64,1024]{2,1,0:T(8,128)(2,1)}), bf16[8,64,1024]{2,1,0:T(8,128)(2,1)S(1)}, u32[]{:S(2)}, u32[]{:S(2)}) async-start(bf16[8,64,1024]{2,1,0:T(8,128)(2,1)} %bitcast.13), calls=%async_computation.3 | async-start | bytes 2097152 | tf_op jit(solution)/shard_map/all_to_all | solution.py:89
Sparse Core Ops, SparseCore 0:
  9.6 37.1 all-gather.2
  48.3 34.4 all-gather.4
  105.2 71.1 reduce-scatter.1
where the time goes:
time: 194 us
  waiting for transfers between devices  87.5 us (45%)
  matrix products  42.2 us (22%)
  starting transfers between devices  19.6 us (10%)
  other arithmetic  16.4 us (8%)
  local copies, waits for them, and re-layouts  13.9 us (7%)
  between operations  13.9 us (7%)
    all_to_all x1, waiting for transfers between devices, per_device(): lax.all_to_all(outgoing.reshape(expert_count, capacity, width), 'expert',...  24.2 us
    all_to_all x1, waiting for transfers between devices, per_device(): lax.all_to_all(grad_back, 'expert', split_axis=0, concat_axis=0, tiled=True)  23.6 us
    all_to_all x1, waiting for transfers between devices, per_device(): lax.all_to_all(grad_cells, 'expert', split_axis=0, concat_axis=0, tiled=T...  19.2 us
    all_to_all x1, waiting for transfers between devices, per_device(): lax.all_to_all(expert_out, 'expert', split_axis=0, concat_axis=0, tiled=T...  19.1 us
    concatenate x1, other arithmetic, per_device(): jnp.concatenate([lax.dot_general(grad_act_buf, expert_rows, (((0,), (0,))...  8.36 us
    dot_general x1, matrix products, per_device(): lax.dot_general(grad_rows, part_out, (((1,), (1,)), ((), ())), preferred_...  7.45 us
    all_to_all x1, starting transfers between devices, per_device(): lax.all_to_all(outgoing.reshape(expert_count, capacity, width), 'expert',...  7.25 us
    dot_general x1, matrix products, per_device(): summed = jnp.dot(hidden, part_out, preferred_element_type=jnp.float32)  7.1 us
  transfers between devices with their start and end apart: 7, of which 4 were waited for; matrix products, arithmetic and copies ran while one was open for 22% of the time, Pallas kernels for 0%

commit v1 on v0

--- a/solution.py
+++ b/solution.py
@@ -17,8 +17,12 @@
     hit_count = jnp.sum(
         (expert_ids[:, :, None] == labels).astype(jnp.int32), axis=1, dtype=jnp.int32
     )
-    earlier = jnp.cumsum(hit_count, axis=0, dtype=jnp.int32) - hit_count
-    slot_ids = jnp.take_along_axis(earlier, expert_ids, axis=1)
+    order = jnp.arange(tok_count, dtype=jnp.int32)
+    before = (order[:, None] > order[None, :]).astype(jnp.bfloat16)
+    earlier = jnp.dot(before, hit_count.astype(jnp.bfloat16), preferred_element_type=jnp.float32)
+    slot_ids = jnp.sum(
+        jnp.where(expert_ids[:, :, None] == labels, earlier[:, None, :], 0.0), axis=2
+    ).astype(jnp.int32)
     target = expert_ids * capacity + slot_ids
     cell_ids = jnp.arange(expert_count * capacity, dtype=jnp.int32)[:, None]
     first_hit = cell_ids == target[:, 0][None, :]

time: 194 us -> 194 us (level)
  local copies, waits for them, and re-layouts: 13.9 us -> 11.3 us
    gather x5 -> x0, local copies, waits for them, and re-layouts: 2.4 us -> none  [per_device(): slot_ids = jnp.take_along_axis(earlier, expert_ids, axis=1)]
    unnamed x13 -> x11, local copies, waits for them, and re-layouts: 6.14 us -> 6.13 us
  transfers between devices with their start and end apart: 7 -> 7, of which waited for: 4 -> 5; matrix products, arithmetic and copies ran while one was open for 22% -> 21% of each run, Pallas kernels for 0% -> 0%
where the time goes in v1:
time: 194 us
  waiting for transfers between devices  89 us (46%)
  matrix products  42.2 us (22%)
  starting transfers between devices  20.2 us (10%)
  other arithmetic  16.9 us (9%)
  between operations  13.9 us (7%)
  local copies, waits for them, and re-layouts  11.3 us (6%)
    all_to_all x1, waiting for transfers between devices, per_device(): lax.all_to_all(outgoing.reshape(expert_count, capacity, width), 'expert',...  24.2 us
    all_to_all x1, waiting for transfers between devices, per_device(): lax.all_to_all(grad_back, 'expert', split_axis=0, concat_axis=0, tiled=True)  23.6 us
    all_to_all x1, waiting for transfers between devices, per_device(): lax.all_to_all(grad_cells, 'expert', split_axis=0, concat_axis=0, tiled=T...  19.4 us
    all_to_all x1, waiting for transfers between devices, per_device(): lax.all_to_all(expert_out, 'expert', split_axis=0, concat_axis=0, tiled=T...  19.1 us
    concatenate x1, other arithmetic, per_device(): jnp.concatenate([lax.dot_general(grad_act_buf, expert_rows, (((0,), (0,))...  8.37 us
    dot_general x1, matrix products, per_device(): lax.dot_general(grad_rows, part_out, (((1,), (1,)), ((), ())), preferred_...  7.47 us
    all_to_all x1, starting transfers between devices, per_device(): lax.all_to_all(outgoing.reshape(expert_count, capacity, width), 'expert',...  7.25 us
    dot_general x1, matrix products, per_device(): summed = jnp.dot(hidden, part_out, preferred_element_type=jnp.float32)  7.1 us
  transfers between devices with their start and end apart: 7, of which 5 were waited for; matrix products, arithmetic and copies ran while one was open for 21% of the time, Pallas kernels for 0%

profile of v1, /device:TPU:0, one launch (start us, length us, event | category | flops | bytes accessed | tf_op | source)
XLA Modules:
  0.0 193.6 jit_solution(5480985136485862991)
XLA Ops:
  10.9 1.4 convolution_convert_fusion.2
  12.3 7.3 %all-to-all-start = ((bf16[8,64,1024]{2,1,0:T(8,128)(2,1)}), bf16[8,64,1024]{2,1,0:T(8,128)(2,1)S(1)}, u32[]{:S(2)}, u32[]{:S(2)}) async-start(bf16[8,64,1024]{2,1,0:T(8,128)(2,1)} %bitcast.2), calls=%async_computation | async-start | bytes 2097152 | tf_op jit(solution)/shard_map/all_to_all | solution.py:37
  19.7 1.4 multiply_convert_fusion
  21.2 24.2 %all-to-all-done = bf16[8,64,1024]{2,1,0:T(8,128)(2,1)S(1)} async-done(((bf16[8,64,1024]{2,1,0:T(8,128)(2,1)}), bf16[8,64,1024]{2,1,0:T(8,128)(2,1)S(1)}, u32[]{:S(2)}, u32[]{:S(2)}) %all-to-all-start) | async-done | bytes 1048608 | tf_op jit(solution)/shard_map/all_to_all | solution.py:37
  45.3 3.6 %all-to-all-start.2 = ((bf16[8,64,1024]{2,1,0:T(8,128)(2,1)}), bf16[8,64,1024]{2,1,0:T(8,128)(2,1)S(1)}, u32[]{:S(2)}, u32[]{:S(2)}) async-start(bf16[8,64,1024]{2,1,0:T(8,128)(2,1)} %bitcast.10), calls=%async_computation.2 | async-start | bytes 2097152 | tf_op jit(solution)/shard_map/all_to_all | solution.py:76
  49.0 6.5 %fusion.23 = f32[512,2048]{1,0:T(8,128)} fusion(bf16[512,1024]{1,0:T(8,128)(2,1)S(1)} %bitcast.46, bf16[1,2048,1024]{2,1,0:T(8,128)(2,1)} %all-gather.3.cloned.1.call-done), kind=kOutput, calls=%fused_computation.31 | convolution fusion | flops 2147483648 | bytes 9437184 | tf_op jit(solution)/shard_map/dot_general | solution.py:53
  55.5 19.4 %all-to-all-done.2 = bf16[8,64,1024]{2,1,0:T(8,128)(2,1)S(1)} async-done(((bf16[8,64,1024]{2,1,0:T(8,128)(2,1)}), bf16[8,64,1024]{2,1,0:T(8,128)(2,1)S(1)}, u32[]{:S(2)}, u32[]{:S(2)}) %all-to-all-start.2) | async-done | bytes 1048608 | tf_op jit(solution)/shard_map/all_to_all | solution.py:76
  74.9 6.7 %convolution_convert_fusion = bf16[2048,1024]{0,1:T(8,128)(2,1)} fusion(bf16[512,1024]{1,0:T(8,128)(2,1)S(1)} %bitcast.48, f32[512,2048]{1,0:T(8,128)} %fusion.23), kind=kOutput, calls=%fused_computation.33 | convolution fusion | flops 2159017984 | bytes 9437184 | tf_op jit(solution)/shard_map/dot_general | solution.py:106
  81.6 1.3 all-gather.5.cloned.1.call-done
  82.9 7.5 %fusion.3 = bf16[512,2048]{1,0:T(8,128)(2,1)S(1)} fusion(bf16[512,1024]{1,0:T(8,128)(2,1)S(1)} %bitcast.49, bf16[1,2048,1024]{2,1,0:T(8,128)(2,1)} %all-gather.5.cloned.1.call-done, f32[512,2048]{1,0:T(8,128)} %fusion.23), kind=kOutput, calls=%fused_computation.11 | convolution fusion | flops 2170552320 | bytes 11534336 | tf_op jit(solution)/shard_map/dot_general | solution.py:85
  91.7 4.4 %convolution_convert_fusion.1 = bf16[2048,1024]{0,1:T(8,128)(2,1)} fusion(bf16[512,2048]{1,0:T(8,128)(2,1)S(1)} %fusion.3, bf16[512,1024]{1,0:T(8,128)(2,1)S(1)} %bitcast.47), kind=kOutput, calls=%fused_computation.34 | convolution fusion | flops 2149580800 | bytes 7340032 | tf_op jit(solution)/shard_map/dot_general | solution.py:100
  96.1 8.4 %pad_maximum_fusion = bf16[2048,2048]{0,1:T(8,128)(2,1)} fusion(bf16[2048,1024]{0,1:T(8,128)(2,1)} %convolution_convert_fusion, bf16[2048,1024]{0,1:T(8,128)(2,1)} %convolution_convert_fusion.1), kind=kLoop, calls=%fused_computation.2 | loop fusion | flops 16777216 | bytes 16777216 | tf_op jit(solution)/shard_map/concatenate | solution.py:98
  104.5 7.1 %fusion.30 = bf16[512,1024]{1,0:T(8,128)(2,1)} fusion(bf16[1,2048,1024]{2,1,0:T(8,128)(2,1)} %all-gather.5.cloned.1.call-done, f32[512,2048]{1,0:T(8,128)} %fusion.23), kind=kOutput, calls=%fused_computation.40 | convolution fusion | flops 2157445120 | bytes 9437184 | tf_op jit(solution)/shard_map/dot_general | solution.py:57
  111.6 5.5 %all-to-all-start.1 = ((bf16[8,64,1024]{2,1,0:T(8,128)(2,1)}), bf16[8,64,1024]{2,1,0:T(8,128)(2,1)S(1)}, u32[]{:S(2)}, u32[]{:S(2)}) async-start(bf16[8,64,1024]{2,1,0:T(8,128)(2,1)} %bitcast.6), calls=%async_computation.1 | async-start | bytes 2097152 | tf_op jit(solution)/shard_map/all_to_all | solution.py:67
  117.1 7.1 %fusion.27 = bf16[512,1024]{1,0:T(8,128)(2,1)} fusion(bf16[512,2048]{1,0:T(8,128)(2,1)} %copy-done.3, bf16[1,2048,1024]{2,1,0:T(8,128)(2,1)} %all-gather.3.cloned.1.call-done), kind=kOutput, calls=%fused_computation.39 | convolution fusion | flops 2148007936 | bytes 7340032 | tf_op jit(solution)/shard_map/dot_general | solution.py:90
  124.2 19.1 %all-to-all-done.1 = bf16[8,64,1024]{2,1,0:T(8,128)(2,1)S(1)} async-done(((bf16[8,64,1024]{2,1,0:T(8,128)(2,1)}), bf16[8,64,1024]{2,1,0:T(8,128)(2,1)S(1)}, u32[]{:S(2)}, u32[]{:S(2)}) %all-to-all-start.1) | async-done | bytes 1048608 | tf_op jit(solution)/shard_map/all_to_all | solution.py:67
  143.2 3.8 %all-to-all-start.3 = ((bf16[8,64,1024]{2,1,0:T(8,128)(2,1)}), bf16[8,64,1024]{2,1,0:T(8,128)(2,1)S(1)}, u32[]{:S(2)}, u32[]{:S(2)}) async-start(bf16[8,64,1024]{2,1,0:T(8,128)(2,1)} %bitcast.12), calls=%async_computation.3 | async-start | bytes 2097152 | tf_op jit(solution)/shard_map/all_to_all | solution.py:93
  149.2 23.6 %all-to-all-done.3 = bf16[8,64,1024]{2,1,0:T(8,128)(2,1)S(1)} async-done(((bf16[8,64,1024]{2,1,0:T(8,128)(2,1)}), bf16[8,64,1024]{2,1,0:T(8,128)(2,1)S(1)}, u32[]{:S(2)}, u32[]{:S(2)}) %all-to-all-start.3) | async-done | bytes 1048608 | tf_op jit(solution)/shard_map/all_to_all | solution.py:93
  174.2 2.1 %reduce_sum.52 = bf16[128,1024]{1,0:T(8,128)(2,1)} reduce(bf16[128,2,1024]{2,1,0:T(2,128)(2,1)S(1)} %reshape.61, bf16[]{:T(256)} %constant.22.clone.1), dimensions={1}, to_apply=%region_4.5 | reduce | flops 131072 | bytes 786434 | tf_op jit(solution)/shard_map/reduce_sum | solution.py:96
  176.3 2.1 %multiply_reduce_fusion = bf16[128,1024]{1,0:T(8,128)(2,1)} fusion(f32[128,2,1024]{2,1,0:T(2,128)S(1)} %reshape.68, f32[128,2]{1,0:T(8,128)S(1)} %copy.22), kind=kLoop, calls=%fused_computation.41 | loop fusion | flops 393216 | bytes 1311744 | tf_op jit(solution)/shard_map/reduce_sum | solution.py:71
  178.4 2.2 %convert_element_type.60 = f32[512,2048]{0,1:T(8,128)S(1)} convert(bf16[512,2048]{0,1:T(8,128)(2,1)} %reduce-scatter.2.cloned.1.call-done) | non-fusion elementwise | flops 1048576 | bytes 6291456 | tf_op jit(solution)/shard_map/convert_element_type | solution.py:118
  180.6 1.8 slice_bitcast_fusion
  182.3 2.9 %copy.23 = f32[1,512,1024]{2,1,0:T(8,128)} copy(f32[1,512,1024]{1,2,0:T(8,128)} %get-tuple-element.19) | data formatting | bytes 4194304
  185.2 1.8 copy.24
  (31 shorter events, 8.8 us)
Async XLA Ops:
  7.2 3.8 %copy-start = (bf16[128,1024]{1,0:T(8,128)(2,1)S(1)}, bf16[128,1024]{1,0:T(8,128)(2,1)}, u32[]{:S(2)}) copy-start(bf16[128,1024]{1,0:T(8,128)(2,1)} %param.6) | copy-start | bytes 786436
  7.2 12.4 %copy-start.2 = (f32[128,2]{0,1:T(2,128)S(1)}, f32[128,2]{0,1:T(2,128)}, u32[]{:S(2)}) copy-start(f32[128,2]{0,1:T(2,128)} %param.8) | copy-start | bytes 3076
  7.2 12.6 %copy-start.1 = (bf16[128,1024]{1,0:T(8,128)(2,1)S(1)}, bf16[128,1024]{1,0:T(8,128)(2,1)}, u32[]{:S(2)}) copy-start(bf16[128,1024]{1,0:T(8,128)(2,1)} %param.11) | copy-start | bytes 786436
  7.2 41.8 %all-gather.3.cloned.1.call-start = ((), (), s32[]{:S(2)}) async-start(), calls=%async_computation.5 | async-start | bytes 5242880 | tf_op jit(solution)/shard_map/all_gather | solution.py:46
  7.9 75.0 %all-gather.5.cloned.1.call-start = ((), (), s32[]{:S(2)}) async-start(), calls=%async_computation.6 | async-start | bytes 5242880 | tf_op jit(solution)/shard_map/all_gather | solution.py:47
  12.3 33.0 %all-to-all-start = ((bf16[8,64,1024]{2,1,0:T(8,128)(2,1)}), bf16[8,64,1024]{2,1,0:T(8,128)(2,1)S(1)}, u32[]{:S(2)}, u32[]{:S(2)}) async-start(bf16[8,64,1024]{2,1,0:T(8,128)(2,1)} %bitcast.2), calls=%async_computation | async-start | bytes 2097152 | tf_op jit(solution)/shard_map/all_to_all | solution.py:37
  45.3 29.5 %all-to-all-start.2 = ((bf16[8,64,1024]{2,1,0:T(8,128)(2,1)}), bf16[8,64,1024]{2,1,0:T(8,128)(2,1)S(1)}, u32[]{:S(2)}, u32[]{:S(2)}) async-start(bf16[8,64,1024]{2,1,0:T(8,128)(2,1)} %bitcast.10), calls=%async_computation.2 | async-start | bytes 2097152 | tf_op jit(solution)/shard_map/all_to_all | solution.py:76
  48.9 129.5 %reduce-scatter.2.cloned.1.call-start = ((), (), s32[]{:S(2)}) async-start(), calls=%async_computation.7 | async-start | bytes 10485760 | tf_op jit(solution)/shard_map/reduce_scatter | solution.py:97
  90.4 1.3 copy-start.3
  111.6 31.7 %all-to-all-start.1 = ((bf16[8,64,1024]{2,1,0:T(8,128)(2,1)}), bf16[8,64,1024]{2,1,0:T(8,128)(2,1)S(1)}, u32[]{:S(2)}, u32[]{:S(2)}) async-start(bf16[8,64,1024]{2,1,0:T(8,128)(2,1)} %bitcast.6), calls=%async_computation.1 | async-start | bytes 2097152 | tf_op jit(solution)/shard_map/all_to_all | solution.py:67
  143.2 29.6 %all-to-all-start.3 = ((bf16[8,64,1024]{2,1,0:T(8,128)(2,1)}), bf16[8,64,1024]{2,1,0:T(8,128)(2,1)S(1)}, u32[]{:S(2)}, u32[]{:S(2)}) async-start(bf16[8,64,1024]{2,1,0:T(8,128)(2,1)} %bitcast.12), calls=%async_computation.3 | async-start | bytes 2097152 | tf_op jit(solution)/shard_map/all_to_all | solution.py:93
Sparse Core Ops, SparseCore 0:
  9.6 37.1 all-gather.2
  48.4 34.4 all-gather.4
  104.6 71.7 reduce-scatter.1

commit v2 on v0

v2 whole, which is shorter than its diff:
```python
import functools
import math

import jax
import jax.numpy as jnp
from jax import lax
from jax.experimental import pallas as pl
from jax.experimental.pallas import tpu as pltpu
from jax.sharding import PartitionSpec as P

F32, BF16 = jnp.float32, jnp.bfloat16
NN = (((1,), (0,)), ((), ()))
NT = (((1,), (1,)), ((), ()))
TN = (((0,), (0,)), ((), ()))


def mul(a, b, dims):
    return lax.dot_general(a, b, dims, preferred_element_type=F32)


def kernel(
    n_f, n_e, cap, steps, depth,
    win, wout, tok, cot, ids, gates,
    layer_out, token_grad, grad_in, grad_out,
    wall, x_send, g_send, x_rows, g_rows, hid, slope, out_acc, dx_acc,
    out_send, dx_send, out_back, dx_back, to_sib, from_sib, to_chip, from_chip, marks,
    load_sem, w_send, w_recv, relay_send, a_send, a_recv, s_send, s_recv, c_send, c_recv,
):
    f, e = lax.axis_index("fsdp"), lax.axis_index("expert")
    chip, core = f // 2, lax.rem(f, 2)
    chips = n_f // 2
    sib = chip * 2 + 1 - core
    count = tok.shape[0]
    cells = n_e * cap

    def over_there(j):
        return lax.rem(chip + j, chips)

    def before(j):
        return lax.rem(chip - j + chips, chips)

    def load(t, a):
        src = win if a == 0 else wout
        return pltpu.make_async_copy(
            src.at[pl.ds(t * depth, depth)], wall.at[f, t, a], load_sem.at[t, a]
        )

    for t in range(steps):
        for a in range(2):
            load(t, a).start()

    barrier = pltpu.get_barrier_semaphore()

    def signal(fi, ei):
        pl.semaphore_signal(
            barrier, inc=1, device_id=(fi, ei), device_id_type=pl.DeviceIdType.MESH
        )

    signal(sib, e)
    for j in range(1, chips):
        signal(over_there(j) * 2 + core, e)

    @pl.loop(1, n_e)
    def _(k):
        signal(f, lax.rem(e + k, n_e))

    def remote(src, dst, send, recv, fi, ei):
        return pltpu.make_async_remote_copy(
            src_ref=src, dst_ref=dst, send_sem=send, recv_sem=recv,
            device_id=(fi, ei), device_id_type=pl.DeviceIdType.MESH,
        )

    def share(t, j):
        to = sib if j == 0 else over_there(j) * 2 + core
        return remote(wall.at[f, t], wall.at[f, t], w_send.at[j, t], w_recv.at[f, t], to, e)

    def arrival(s, t):
        return remote(wall.at[s, t], wall.at[s, t], w_send.at[0, t], w_recv.at[s, t], sib, e)

    def relay(s, t, j):
        return remote(wall.at[s, t], wall.at[s, t], relay_send.at[j, t], w_recv.at[s, t], sib, e)

    pl.semaphore_wait(barrier, 1 + (chips - 1) + (n_e - 1))
    for t in range(steps):
        for a in range(2):
            load(t, a).wait()
        for j in range(1, chips):
            share(t, j).start()
        share(t, 0).start()

    lanes = lax.broadcasted_iota(jnp.int32, (count, 128), 1)
    first, second = ids[:, 0:1], ids[:, 1:2]
    hit = (lanes == first).astype(F32) + (lanes == second).astype(F32)
    earlier_than = (
        lax.broadcasted_iota(jnp.int32, (count, count), 0)
        > lax.broadcasted_iota(jnp.int32, (count, count), 1)
    ).astype(F32)
    earlier = mul(earlier_than.astype(BF16), hit.astype(BF16), NN)
    spots = lax.broadcasted_iota(jnp.int32, (count, cells), 1)
    gate_at = jnp.zeros((count, cells), F32)
    placed = jnp.zeros((count, cells), F32)
    for k, chosen in enumerate((first, second)):
        slot = jnp.sum(jnp.where(lanes == chosen, earlier, 0.0), axis=1, keepdims=True)
        here = spots == chosen * cap + slot.astype(jnp.int32)
        marks[k] = here.astype(F32).astype(BF16)
        placed += here.astype(F32)
        gate_at += jnp.where(here, gates[:, k : k + 1], 0.0)
    placing = placed.T.astype(BF16)
    gate_cells = jnp.sum(gate_at.T, axis=1, keepdims=True)

    def part(buf, i):
        return buf.at[pl.ds(pl.multiple_of(i * cap, cap), cap)]

    def exchange(a, src, dst, k):
        to = lax.rem(e + k, n_e)
        return remote(part(src, to), part(dst, e), a_send.at[a, k], a_recv.at[a, k], f, to)

    def arriving(a, src, dst, k):
        frm = lax.rem(e - k + n_e, n_e)
        return remote(part(src, frm), part(dst, frm), a_send.at[a, k], a_recv.at[a, k], f, frm)

    def send_all(a, src, dst):
        @pl.loop(1, n_e)
        def _(k):
            exchange(a, src, dst, k).start()

        own = pl.ds(pl.multiple_of(e * cap, cap), cap)
        dst[own, :] = src[own, :]

    def receive_all(a, src, dst):
        @pl.loop(1, n_e)
        def _(k):
            arriving(a, src, dst, k).wait_recv()

    def sent_all(a, src, dst):
        @pl.loop(1, n_e)
        def _(k):
            exchange(a, src, dst, k).wait_send()

    x_send[...] = mul(placing, tok[...], NN).astype(BF16)
    send_all(0, x_send, x_rows)
    g_send[...] = (mul(placing, cot[...], NN) * gate_cells).astype(BF16)
    send_all(1, g_send, g_rows)
    out_acc[...] = jnp.zeros_like(out_acc)
    dx_acc[...] = jnp.zeros_like(dx_acc)

    scale = math.sqrt(2.0 / math.pi)

    def forward(s, t):
        pre = mul(x_rows[...], wall[s, t, 0], NT)
        square = pre * pre
        th = jnp.tanh(scale * pre * (1.0 + 0.044715 * square))
        half = 0.5 * (1.0 + th)
        hidden = (pre * half).astype(BF16)
        hid[s, t] = hidden
        slope[s, t] = half + 0.5 * pre * (1.0 - th * th) * (
            scale * (1.0 + 3.0 * 0.044715 * square)
        )
        out_acc[...] += mul(hidden, wall[s, t, 1], NN)

    receive_all(0, x_send, x_rows)

    @pl.loop(0, steps)
    def _(t):
        forward(f, t)

    @pl.loop(0, steps)
    def _(t):
        arrival(sib, t).wait_recv()
        forward(sib, t)

    @pl.loop(1, chips)
    def _(j):
        s = over_there(j) * 2 + core

        @pl.loop(0, steps)
        def _(t):
            arrival(s, t).wait_recv()
            relay(s, t, j).start()
            forward(s, t)

    @pl.loop(1, chips)
    def _(j):
        s = over_there(j) * 2 + 1 - core

        @pl.loop(0, steps)
        def _(t):
            arrival(s, t).wait_recv()
            forward(s, t)

    out_send[...] = out_acc[...].astype(BF16)
    send_all(2, out_send, out_back)

    def backward(s, t):
        d_hidden = mul(g_rows[...], wall[s, t, 1], NT)
        d_pre = (d_hidden * slope[s, t]).astype(BF16)
        dx_acc[...] += mul(d_pre, wall[s, t, 0], NN)
        return mul(d_pre, x_rows[...], TN), mul(hid[s, t], g_rows[...], TN)

    def to_sibling(j, t):
        return remote(to_sib.at[j, t], from_sib.at[j, t], s_send.at[j, t], s_recv.at[j, t], sib, e)

    def across(j, t):
        to = over_there(j) * 2 + core
        return remote(to_chip.at[j, t], from_chip.at[j, t], c_send.at[j, t], c_recv.at[j, t], to, e)

    def across_in(j, t):
        frm = before(j) * 2 + core
        return remote(to_chip.at[j, t], from_chip.at[j, t], c_send.at[j, t], c_recv.at[j, t], frm, e)

    receive_all(1, g_send, g_rows)

    def siblings(j):
        s = over_there(j) * 2 + 1 - core

        @pl.loop(0, steps)
        def _(t):
            g_in, g_out = backward(s, t)
            to_sib[j, t, 0] = g_in.astype(BF16)
            to_sib[j, t, 1] = g_out.astype(BF16)
            to_sibling(j, t).start()

    @pl.loop(1, chips)
    def _(j):
        siblings(j)

    @pl.loop(1, chips)
    def _(j):
        s = over_there(j) * 2 + core

        @pl.loop(0, steps)
        def _(t):
            g_in, g_out = backward(s, t)
            to_sibling(j, t).wait_recv()
            to_chip[j, t, 0] = (g_in + from_sib[j, t, 0].astype(F32)).astype(BF16)
            to_chip[j, t, 1] = (g_out + from_sib[j, t, 1].astype(F32)).astype(BF16)
            across(j, t).start()

    siblings(0)

    @pl.loop(0, steps)
    def _(t):
        g_in, g_out = backward(f, t)
        rows = pl.ds(pl.multiple_of(t * depth, depth), depth)
        grad_in[rows, :] = g_in
        grad_out[rows, :] = g_out

    dx_send[...] = dx_acc[...].astype(BF16)
    send_all(3, dx_send, dx_back)

    @pl.loop(0, steps)
    def _(t):
        to_sibling(0, t).wait_recv()
        rows = pl.ds(pl.multiple_of(t * depth, depth), depth)
        grad_in[rows, :] += from_sib[0, t, 0].astype(F32)
        grad_out[rows, :] += from_sib[0, t, 1].astype(F32)

    receive_all(2, out_send, out_back)
    layer_out[...] = (
        mul(marks[0], out_back[...], NN) * gates[:, 0:1]
        + mul(marks[1], out_back[...], NN) * gates[:, 1:2]
    ).astype(BF16)

    @pl.loop(1, chips)
    def _(j):
        @pl.loop(0, steps)
        def _(t):
            across_in(j, t).wait_recv()
            rows = pl.ds(pl.multiple_of(t * depth, depth), depth)
            grad_in[rows, :] += from_chip[j, t, 0].astype(F32)
            grad_out[rows, :] += from_chip[j, t, 1].astype(F32)

    receive_all(3, dx_send, dx_back)
    token_grad[...] = (
        mul(marks[0], dx_back[...], NN) + mul(marks[1], dx_back[...], NN)
    ).astype(BF16)

    for a, (src, dst) in enumerate(
        ((x_send, x_rows), (g_send, g_rows), (out_send, out_back), (dx_send, dx_back))
    ):
        sent_all(a, src, dst)
    for t in range(steps):
        for j in range(chips):
            share(t, j).wait_send()
            to_sibling(j, t).wait_send()
        for j in range(1, chips):
            relay(over_there(j) * 2 + core, t, j).wait_send()
            across(j, t).wait_send()


def per_device(tokens, expert_ids, gate_weights, weight_in, weight_out, cotangent):
    count, width = tokens.shape
    n_f, n_e = lax.axis_size("fsdp"), lax.axis_size("expert")
    cap = 4 * count // n_e
    owned = weight_in.shape[1]
    depth = min(256, owned)
    steps = owned // depth
    rows, chips = n_e * cap, n_f // 2
    vmem = pl.BlockSpec(memory_space=pltpu.VMEM)
    anywhere = pl.BlockSpec(memory_space=pl.ANY)
    dma = pltpu.SemaphoreType.DMA
    wide = pltpu.VMEM((rows, width), BF16)
    total = pltpu.VMEM((rows, width), F32)
    pieces = pltpu.VMEM((chips, steps, 2, depth, width), BF16)
    flops = 12 * rows * width * owned * n_f
    layer_out, token_grad, grad_in, grad_out = pl.pallas_call(
        functools.partial(kernel, n_f, n_e, cap, steps, depth),
        out_shape=(
            jax.ShapeDtypeStruct((count, width), BF16),
            jax.ShapeDtypeStruct((count, width), BF16),
            jax.ShapeDtypeStruct((owned, width), F32),
            jax.ShapeDtypeStruct((owned, width), F32),
        ),
        in_specs=[anywhere, anywhere, vmem, vmem, vmem, vmem],
        out_specs=(vmem, vmem, vmem, vmem),
        scratch_shapes=[
            pltpu.VMEM((n_f, steps, 2, depth, width), BF16),
            wide, wide, wide, wide,
            pltpu.VMEM((n_f, steps, rows, depth), BF16),
            pltpu.VMEM((n_f, steps, rows, depth), F32),
            total, total,
            wide, wide, wide, wide,
            pieces, pieces, pieces, pieces,
            pltpu.VMEM((2, count, rows), BF16),
            dma((steps, 2)),
            dma((chips, steps)),
            dma((n_f, steps)),
            dma((chips, steps)),
            dma((4, n_e)),
            dma((4, n_e)),
            dma((chips, steps)),
            dma((chips, steps)),
            dma((chips, steps)),
            dma((chips, steps)),
        ],
        compiler_params=pltpu.CompilerParams(
            collective_id=0, has_side_effects=True, vmem_limit_bytes=58 * 2**20
        ),
        cost_estimate=pl.CostEstimate(
            flops=flops, bytes_accessed=16 * owned * width, transcendentals=rows * owned * n_f
        ),
    )(weight_in[0], weight_out[0], tokens, cotangent, expert_ids, gate_weights)
    return layer_out, token_grad, grad_in[None], grad_out[None]


def solution(mesh):
    tok, weight = P(("fsdp", "expert"), None), P("expert", "fsdp", None)
    return jax.shard_map(
        per_device,
        mesh=mesh,
        in_specs=(tok, tok, tok, weight, weight, tok),
        out_specs=(tok, tok, weight, weight),
        check_vma=False,
    )
```

time: 194 us -> 126 us (0.65)
  Pallas kernels: 0 us -> 114 us
  waiting for transfers between devices: 87.5 us -> 0 us
  matrix products: 42.2 us -> 0 us
  starting transfers between devices: 19.6 us -> 0 us
  other arithmetic: 16.4 us -> 0 us
  between operations: 13.9 us -> 0.64 us
  local copies, waits for them, and re-layouts: 13.9 us -> 10.8 us
    pallas_call x0 -> x1, Pallas kernels: none -> 114 us  [per_device(): pl.pallas_call(functools.partial(kernel, n_f, n_e, cap, steps, depth), ou...]
    all_to_all x4 -> x0, waiting for transfers between devices: 86.1 us -> none  [the longest x1 24.2 us: per_device(): lax.all_to_all(outgoing.reshape(expert_count, capacity, width), 'expert',...]
    dot_general x8 -> x0, matrix products: 42.2 us -> none  [the longest x1 7.45 us: per_device(): lax.dot_general(grad_rows, part_out, (((1,), (1,)), ((), ())), preferred_...]
    all_to_all x4 -> x0, starting transfers between devices: 19.5 us -> none  [the longest x1 7.25 us: per_device(): lax.all_to_all(outgoing.reshape(expert_count, capacity, width), 'expert',...]
    concatenate x1 -> x0, other arithmetic: 8.36 us -> none  [per_device(): jnp.concatenate([lax.dot_general(grad_act_buf, expert_rows, (((0,), (0,))...]
    reduce_sum x4 -> x0, other arithmetic: 5 us -> none  [the longest x1 2.08 us: per_device(): jnp.sum(grad_returned[target].astype(jnp.float32), axis=1)]
    gather x8 -> x0, local copies, waits for them, and re-layouts: 4.93 us -> none  [the longest x5 2.4 us: per_device(): slot_ids = jnp.take_along_axis(earlier, expert_ids, axis=1)]
    unnamed x13 -> x8, local copies, waits for them, and re-layouts: 6.14 us -> 10.8 us
  transfers between devices with their start and end apart: 7 -> 0, of which waited for: 4 -> 0; matrix products, arithmetic and copies ran while one was open for 22% -> 0% of each run, Pallas kernels for 0% -> 0%
where the time goes in v2:
time: 126 us
  Pallas kernels  114 us (90%)
  local copies, waits for them, and re-layouts  10.8 us (9%)
    pallas_call x1, Pallas kernels, per_device(): pl.pallas_call(functools.partial(kernel, n_f, n_e, cap, steps, depth), ou...  114 us
    unnamed x8, local copies, waits for them, and re-layouts  10.8 us

profile of v2, /device:TPU:0, one launch (start us, length us, event | category | flops | bytes accessed | tf_op | source)
XLA Modules:
  0.0 125.6 jit_solution(3606958494157608599)
XLA Ops:
  0.6 1.4 %copy.10.ids = s32[128,2]{1,0:T(8,128)} copy(s32[128,2]{0,1:T(2,128)} %param.7) | data formatting | bytes 2048 | tf_op args[1]
  2.0 1.4 %copy.11.gates = f32[128,2]{1,0:T(8,128)} copy(f32[128,2]{0,1:T(2,128)} %param.8) | data formatting | bytes 2048 | tf_op args[2]
  3.5 114.1 %shard_map.93 = (bf16[128,1024]{1,0:T(8,128)(2,1)}, bf16[128,1024]{1,0:T(8,128)(2,1)}, f32[512,1024]{1,0:T(8,128)}, f32[512,1024]{1,0:T(8,128)}) custom-call(bf16[512,1024]{1,0:T(8,128)(2,1)} %bitcast.6, bf16[512,1024]{1,0:T(8,128)(2,1)} %bitcast.7, bf16[128,1024]{1,0:T(8,128)(2,1)} %tok.1, bf16[128,1024]{1,0:T(8,128)(2,1)} %cot.1, s32[128,2]{1,0:T(8,128)} %copy.10.ids, ...), custom_call_target="tpu_custom_call" | custom-call | flops 12884901888 | bytes 8388608 | tf_op jit(solution)/shard_map/pallas_call | solution.py:306
  117.6 1.7 %copy.16 = bf16[128,1024]{1,0:T(8,128)(2,1)} copy(bf16[128,1024]{1,0:T(8,128)(2,1)} %get-tuple-element.16) | data formatting | bytes 524288
  119.3 1.7 %copy.17 = bf16[128,1024]{1,0:T(8,128)(2,1)} copy(bf16[128,1024]{1,0:T(8,128)(2,1)} %get-tuple-element.17) | data formatting | bytes 524288
  120.9 0.0 copy-start
  120.9 3.3 %copy.18 = f32[1,512,1024]{2,1,0:T(8,128)} copy(f32[1,512,1024]{2,1,0:T(8,128)} %bitcast.5) | data formatting | bytes 4194304
  124.2 0.0 copy-done
  124.2 1.3 %copy.19 = f32[1,512,1024]{2,1,0:T(8,128)} copy(f32[1,512,1024]{2,1,0:T(8,128)S(1)} %bitcast.4) | data formatting | bytes 4194304
Async XLA Ops:
  120.9 3.3 %copy-start = (f32[512,1024]{1,0:T(8,128)S(1)}, f32[512,1024]{1,0:T(8,128)}, u32[]{:S(2)}) copy-start(f32[512,1024]{1,0:T(8,128)} %get-tuple-element.11) | copy-start | bytes 6291460

commit v3 on v2

--- a/solution.py
+++ b/solution.py
@@ -18,12 +18,16 @@
     return lax.dot_general(a, b, dims, preferred_element_type=F32)
 
 
+def upright(rows):
+    return jnp.concatenate([rows, jnp.zeros((6, rows.shape[1]), rows.dtype)], axis=0).T
+
+
 def kernel(
     n_f, n_e, cap, steps, depth,
     win, wout, tok, cot, ids, gates,
     layer_out, token_grad, grad_in, grad_out,
     wall, x_send, g_send, x_rows, g_rows, hid, slope, out_acc, dx_acc,
-    out_send, dx_send, out_back, dx_back, to_sib, from_sib, to_chip, from_chip, marks,
+    out_send, dx_send, out_back, dx_back, to_sib, from_sib, to_chip, from_chip, marks, gate_at_token, slopes_on,
     load_sem, w_send, w_recv, relay_send, a_send, a_recv, s_send, s_recv, c_send, c_recv,
 ):
     f, e = lax.axis_index("fsdp"), lax.axis_index("expert")
@@ -80,16 +84,9 @@
     def relay(s, t, j):
         return remote(wall.at[s, t], wall.at[s, t], relay_send.at[j, t], w_recv.at[s, t], sib, e)
 
-    pl.semaphore_wait(barrier, 1 + (chips - 1) + (n_e - 1))
-    for t in range(steps):
-        for a in range(2):
-            load(t, a).wait()
-        for j in range(1, chips):
-            share(t, j).start()
-        share(t, 0).start()
-
+    ids_at, gate_at_token[...] = upright(ids[...].astype(F32)), upright(gates[...])
     lanes = lax.broadcasted_iota(jnp.int32, (count, 128), 1)
-    first, second = ids[:, 0:1], ids[:, 1:2]
+    first, second = ids_at[:, 0:1].astype(jnp.int32), ids_at[:, 1:2].astype(jnp.int32)
     hit = (lanes == first).astype(F32) + (lanes == second).astype(F32)
     earlier_than = (
         lax.broadcasted_iota(jnp.int32, (count, count), 0)
@@ -104,7 +101,7 @@
         here = spots == chosen * cap + slot.astype(jnp.int32)
         marks[k] = here.astype(F32).astype(BF16)
         placed += here.astype(F32)
-        gate_at += jnp.where(here, gates[:, k : k + 1], 0.0)
+        gate_at += jnp.where(here, gate_at_token[:, k : k + 1], 0.0)
     placing = placed.T.astype(BF16)
     gate_cells = jnp.sum(gate_at.T, axis=1, keepdims=True)
 
@@ -138,9 +135,23 @@
             exchange(a, src, dst, k).wait_send()
 
     x_send[...] = mul(placing, tok[...], NN).astype(BF16)
+    pl.semaphore_wait(barrier, 1 + (chips - 1) + (n_e - 1))
+    for t in range(steps):
+        for a in range(2):
+            load(t, a).wait()
+        for j in range(1, chips):
+            share(t, j).start()
+        share(t, 0).start()
     send_all(0, x_send, x_rows)
     g_send[...] = (mul(placing, cot[...], NN) * gate_cells).astype(BF16)
-    send_all(1, g_send, g_rows)
+
+    @pl.loop(1, n_e)
+    def _(k):
+        exchange(0, x_send, x_rows, k).wait_send()
+        exchange(1, g_send, g_rows, k).start()
+
+    own_cells = pl.ds(pl.multiple_of(e * cap, cap), cap)
+    g_rows[own_cells, :] = g_send[own_cells, :]
     out_acc[...] = jnp.zeros_like(out_acc)
     dx_acc[...] = jnp.zeros_like(dx_acc)
 
@@ -169,33 +180,33 @@
         arrival(sib, t).wait_recv()
         forward(sib, t)
 
+    def take(j, t):
+        s = over_there(j) * 2 + core
+        arrival(s, t).wait_recv()
+        relay(s, t, j).start()
+
+    def forward_there(j, t):
+        forward(over_there(j) * 2 + core, t)
+        s = over_there(j) * 2 + 1 - core
+        arrival(s, t).wait_recv()
+        forward(s, t)
+
     @pl.loop(1, chips)
     def _(j):
-        s = over_there(j) * 2 + core
-
-        @pl.loop(0, steps)
-        def _(t):
-            arrival(s, t).wait_recv()
-            relay(s, t, j).start()
-            forward(s, t)
-
-    @pl.loop(1, chips)
-    def _(j):
-        s = over_there(j) * 2 + 1 - core
-
-        @pl.loop(0, steps)
-        def _(t):
-            arrival(s, t).wait_recv()
-            forward(s, t)
-
-    out_send[...] = out_acc[...].astype(BF16)
-    send_all(2, out_send, out_back)
-
-    def backward(s, t):
+        take(j, 0)
+        forward_there(j, 0)
+
+    def back(s, t):
         d_hidden = mul(g_rows[...], wall[s, t, 1], NT)
         d_pre = (d_hidden * slope[s, t]).astype(BF16)
         dx_acc[...] += mul(d_pre, wall[s, t, 0], NN)
+        return d_pre
+
+    def weight_grads(s, t, d_pre):
         return mul(d_pre, x_rows[...], TN), mul(hid[s, t], g_rows[...], TN)
+
+    def backward(s, t):
+        return weight_grads(s, t, back(s, t))
 
     def to_sibling(j, t):
         return remote(to_sib.at[j, t], from_sib.at[j, t], s_send.at[j, t], s_recv.at[j, t], sib, e)
@@ -208,45 +219,65 @@
         frm = before(j) * 2 + core
         return remote(to_chip.at[j, t], from_chip.at[j, t], c_send.at[j, t], c_recv.at[j, t], frm, e)
 
+    def pass_on(j, t, g_in, g_out):
+        to_sib[j, t, 0] = g_in.astype(BF16)
+        to_sib[j, t, 1] = g_out.astype(BF16)
+        to_sibling(j, t).start()
+
+    def backward_there(j, t):
+        g_in, g_out = backward(over_there(j) * 2 + 1 - core, t)
+        pass_on(j, t, g_in, g_out)
+        g_in, g_out = backward(over_there(j) * 2 + core, t)
+        to_sibling(j, t).wait_recv()
+        to_chip[j, t, 0] = (g_in + from_sib[j, t, 0].astype(F32)).astype(BF16)
+        to_chip[j, t, 1] = (g_out + from_sib[j, t, 1].astype(F32)).astype(BF16)
+        across(j, t).start()
+
     receive_all(1, g_send, g_rows)
-
-    def siblings(j):
-        s = over_there(j) * 2 + 1 - core
-
-        @pl.loop(0, steps)
-        def _(t):
-            g_in, g_out = backward(s, t)
-            to_sib[j, t, 0] = g_in.astype(BF16)
-            to_sib[j, t, 1] = g_out.astype(BF16)
-            to_sibling(j, t).start()
 
     @pl.loop(1, chips)
     def _(j):
-        siblings(j)
-
-    @pl.loop(1, chips)
-    def _(j):
-        s = over_there(j) * 2 + core
+        backward_there(j, 0)
+
+    @pl.loop(1, steps)
+    def _(t):
+        @pl.loop(1, chips)
+        def _(j):
+            take(j, t)
+
+        @pl.loop(1, chips)
+        def _(j):
+            forward_there(j, t)
+
+    out_send[...] = out_acc[...].astype(BF16)
+    send_all(2, out_send, out_back)
+
+    @pl.loop(1, steps)
+    def _(t):
+        @pl.loop(1, chips)
+        def _(j):
+            backward_there(j, t)
+
+    for i, s in enumerate((sib, f)):
 
         @pl.loop(0, steps)
-        def _(t):
-            g_in, g_out = backward(s, t)
-            to_sibling(j, t).wait_recv()
-            to_chip[j, t, 0] = (g_in + from_sib[j, t, 0].astype(F32)).astype(BF16)
-            to_chip[j, t, 1] = (g_out + from_sib[j, t, 1].astype(F32)).astype(BF16)
-            across(j, t).start()
-
-    siblings(0)
+        def _(t, i=i, s=s):
+            slopes_on[i, t] = back(s, t)
+
+    dx_send[...] = dx_acc[...].astype(BF16)
+    send_all(3, dx_send, dx_back)
 
     @pl.loop(0, steps)
     def _(t):
-        g_in, g_out = backward(f, t)
+        g_in, g_out = weight_grads(sib, t, slopes_on[0, t])
+        pass_on(0, t, g_in, g_out)
+
+    @pl.loop(0, steps)
+    def _(t):
+        g_in, g_out = weight_grads(f, t, slopes_on[1, t])
         rows = pl.ds(pl.multiple_of(t * depth, depth), depth)
         grad_in[rows, :] = g_in
         grad_out[rows, :] = g_out
-
-    dx_send[...] = dx_acc[...].astype(BF16)
-    send_all(3, dx_send, dx_back)
 
     @pl.loop(0, steps)
     def _(t):
@@ -257,8 +288,8 @@
 
     receive_all(2, out_send, out_back)
     layer_out[...] = (
-        mul(marks[0], out_back[...], NN) * gates[:, 0:1]
-        + mul(marks[1], out_back[...], NN) * gates[:, 1:2]
+        mul(marks[0], out_back[...], NN) * gate_at_token[:, 0:1]
+        + mul(marks[1], out_back[...], NN) * gate_at_token[:, 1:2]
     ).astype(BF16)
 
     @pl.loop(1, chips)
@@ -275,10 +306,9 @@
         mul(marks[0], dx_back[...], NN) + mul(marks[1], dx_back[...], NN)
     ).astype(BF16)
 
-    for a, (src, dst) in enumerate(
-        ((x_send, x_rows), (g_send, g_rows), (out_send, out_back), (dx_send, dx_back))
-    ):
-        sent_all(a, src, dst)
+    sent_all(1, g_send, g_rows)
+    sent_all(2, out_send, out_back)
+    sent_all(3, dx_send, dx_back)
     for t in range(steps):
         for j in range(chips):
             share(t, j).wait_send()
@@ -286,6 +316,21 @@
         for j in range(1, chips):
             relay(over_there(j) * 2 + core, t, j).wait_send()
             across(j, t).wait_send()
+
+
+def settle(cuts, sources, targets, sems):
+    copies = []
+    for i, (src, dst) in enumerate(zip(sources, targets)):
+        rows = src.shape[0] // cuts[i]
+        for c in range(cuts[i]):
+            part = pl.ds(c * rows, rows)
+            copies.append(
+                pltpu.make_async_copy(src.at[part], dst.at[part], sems.at[len(copies)])
+            )
+    for copy in copies:
+        copy.start()
+    for copy in copies:
+        copy.wait()
 
 
 def per_device(tokens, expert_ids, gate_weights, weight_in, weight_out, cotangent):
@@ -322,6 +367,8 @@
             wide, wide, wide, wide,
             pieces, pieces, pieces, pieces,
             pltpu.VMEM((2, count, rows), BF16),
+            pltpu.VMEM((count, 8), F32),
+            pltpu.VMEM((2, steps, rows, depth), BF16),
             dma((steps, 2)),
             dma((chips, steps)),
             dma((n_f, steps)),
@@ -339,7 +386,16 @@
         cost_estimate=pl.CostEstimate(
             flops=flops, bytes_accessed=16 * owned * width, transcendentals=rows * owned * n_f
         ),
-    )(weight_in[0], weight_out[0], tokens, cotangent, expert_ids, gate_weights)
+    )(weight_in[0], weight_out[0], tokens, cotangent, expert_ids.T, gate_weights.T)
+    results = (layer_out, token_grad, grad_in, grad_out)
+    cuts = (1, 1, 4, 4)
+    layer_out, token_grad, grad_in, grad_out = pl.pallas_call(
+        lambda *refs: settle(cuts, refs[:4], refs[4:8], refs[8]),
+        out_shape=tuple(jax.ShapeDtypeStruct(r.shape, r.dtype) for r in results),
+        in_specs=[anywhere] * 4,
+        out_specs=(anywhere,) * 4,
+        scratch_shapes=[dma((sum(cuts),))],
+    )(*results)
     return layer_out, token_grad, grad_in[None], grad_out[None]
 
 

time: 126 us -> 254 us (2.02)
  the two profiles are of different devices: /device:TPU:0 before, /device:TPU:26 now
where the time goes in v3:
time: 254 us
  Pallas kernels  253 us (100%)
    pallas_call x1, Pallas kernels, per_device(): pl.pallas_call(lambda *refs: settle(cuts, refs[:4], refs[4:8], refs[8]),...  144 us
    pallas_call x1, Pallas kernels, per_device(): pl.pallas_call(functools.partial(kernel, n_f, n_e, cap, steps, depth), ou...  109 us

profile of v3, /device:TPU:26, one launch (start us, length us, event | category | flops | bytes accessed | tf_op | source)
XLA Modules:
  0.0 253.8 jit_solution(7418411136718589811)
XLA Ops:
  0.6 108.9 %shard_map.93 = (bf16[128,1024]{1,0:T(8,128)(2,1)}, bf16[128,1024]{1,0:T(8,128)(2,1)}, f32[512,1024]{1,0:T(8,128)}, f32[512,1024]{1,0:T(8,128)}) custom-call(bf16[512,1024]{1,0:T(8,128)(2,1)} %bitcast.8, bf16[512,1024]{1,0:T(8,128)(2,1)} %bitcast.9, bf16[128,1024]{1,0:T(8,128)(2,1)} %tok.1, bf16[128,1024]{1,0:T(8,128)(2,1)} %cot.1, s32[2,128]{1,0:T(2,128)} %bitcast.10, ...), custom_call_target="tpu_custom_call" | custom-call | flops 12884901888 | bytes 8388608 | tf_op jit(solution)/shard_map/pallas_call | solution.py:351
  109.5 144.1 %shard_map.94 = (bf16[128,1024]{1,0:T(8,128)(2,1)}, bf16[128,1024]{1,0:T(8,128)(2,1)}, f32[512,1024]{1,0:T(8,128)}, f32[512,1024]{1,0:T(8,128)}) custom-call(bf16[128,1024]{1,0:T(8,128)(2,1)} %get-tuple-element.12.refs_0_, bf16[128,1024]{1,0:T(8,128)(2,1)} %get-tuple-element.13.refs_1_, f32[512,1024]{1,0:T(8,128)} %get-tuple-element.14.refs_2_, ...), custom_call_target="tpu_custom_call" | custom-call | tf_op jit(solution)/shard_map/pallas_call | solution.py:392

commit v4 on v3

--- a/solution.py
+++ b/solution.py
@@ -318,19 +318,9 @@
             across(j, t).wait_send()
 
 
-def settle(cuts, sources, targets, sems):
-    copies = []
-    for i, (src, dst) in enumerate(zip(sources, targets)):
-        rows = src.shape[0] // cuts[i]
-        for c in range(cuts[i]):
-            part = pl.ds(c * rows, rows)
-            copies.append(
-                pltpu.make_async_copy(src.at[part], dst.at[part], sems.at[len(copies)])
-            )
-    for copy in copies:
-        copy.start()
-    for copy in copies:
-        copy.wait()
+def settle(*refs):
+    for src, dst in zip(refs[:4], refs[4:]):
+        dst[...] = src[...]
 
 
 def per_device(tokens, expert_ids, gate_weights, weight_in, weight_out, cotangent):
@@ -388,13 +378,13 @@
         ),
     )(weight_in[0], weight_out[0], tokens, cotangent, expert_ids.T, gate_weights.T)
     results = (layer_out, token_grad, grad_in, grad_out)
-    cuts = (1, 1, 4, 4)
+    blocks = [pl.BlockSpec((r.shape[0] // 4, width), lambda i: (i, 0)) for r in results]
     layer_out, token_grad, grad_in, grad_out = pl.pallas_call(
-        lambda *refs: settle(cuts, refs[:4], refs[4:8], refs[8]),
+        settle,
+        grid=(4,),
         out_shape=tuple(jax.ShapeDtypeStruct(r.shape, r.dtype) for r in results),
-        in_specs=[anywhere] * 4,
-        out_specs=(anywhere,) * 4,
-        scratch_shapes=[dma((sum(cuts),))],
+        in_specs=blocks,
+        out_specs=tuple(blocks),
     )(*results)
     return layer_out, token_grad, grad_in[None], grad_out[None]
 

time: 254 us -> 115 us (0.45)
  Pallas kernels: 253 us -> 114 us
    pallas_call x1, Pallas kernels: 144 us -> 5.02 us  [per_device(): pl.pallas_call(settle, grid=(4,), out_shape=tuple((jax.ShapeDtypeStruct(r...]
where the time goes in v4:
time: 115 us
  Pallas kernels  114 us (99%)
    pallas_call x1, Pallas kernels, per_device(): pl.pallas_call(functools.partial(kernel, n_f, n_e, cap, steps, depth), ou...  109 us
    pallas_call x1, Pallas kernels, per_device(): pl.pallas_call(settle, grid=(4,), out_shape=tuple((jax.ShapeDtypeStruct(r...  5.02 us

profile of v4, /device:TPU:26, one launch (start us, length us, event | category | flops | bytes accessed | tf_op | source)
XLA Modules:
  0.0 114.5 jit_solution(16136096889375559892)
XLA Ops:
  0.6 108.9 %shard_map.93 = (bf16[128,1024]{1,0:T(8,128)(2,1)}, bf16[128,1024]{1,0:T(8,128)(2,1)}, f32[512,1024]{1,0:T(8,128)}, f32[512,1024]{1,0:T(8,128)}) custom-call(bf16[512,1024]{1,0:T(8,128)(2,1)} %bitcast.8, bf16[512,1024]{1,0:T(8,128)(2,1)} %bitcast.9, bf16[128,1024]{1,0:T(8,128)(2,1)} %tok.1, bf16[128,1024]{1,0:T(8,128)(2,1)} %cot.1, s32[2,128]{1,0:T(2,128)} %bitcast.10, ...), custom_call_target="tpu_custom_call" | custom-call | flops 12884901888 | bytes 8388608 | tf_op jit(solution)/shard_map/pallas_call | solution.py:341
  109.5 5.0 %shard_map.94 = (bf16[128,1024]{1,0:T(8,128)(2,1)}, bf16[128,1024]{1,0:T(8,128)(2,1)}, f32[512,1024]{1,0:T(8,128)}, f32[512,1024]{1,0:T(8,128)}) custom-call(bf16[128,1024]{1,0:T(8,128)(2,1)} %get-tuple-element.12.refs_0_, bf16[128,1024]{1,0:T(8,128)(2,1)} %get-tuple-element.13.refs_1_, f32[512,1024]{1,0:T(8,128)} %get-tuple-element.14.refs_2_, ...), custom_call_target="tpu_custom_call" | custom-call | tf_op jit(solution)/shard_map/pallas_call | solution.py:382
